TPU v7x, 128 devices: a whole 4x4x4 slice. The times are simulated.
128 devices in a mesh: group: 4 (over y), pos: 32 (over x, z, core).
Axes of the slice: x: 4, y: 4, z: 4, core: 2. Of those that a mesh axis runs over, the one named last changes fastest.
Arguments:
- cand_x: bfloat16 [4, 16384, 1024], P('group', 'pos'), may hold values from -6 to 6
- f1_weight: bfloat16 [1024, 4096], replicated, may hold values from -0.1875 to 0.1875
- out_weight: bfloat16 [1024, 1024], replicated, may hold values from -0.1875 to 0.1875
- kv_cache: bfloat16 [4, 4096, 2048], P('group', 'pos'), may hold values from -6 to 6
- user_slot: int32 [4], replicated, may hold values from 0 to 3, each once
- hist_len: int32 [4], replicated, may hold values from 128 to 4096, as said below
- cand_count: int32 [4], replicated, may hold values from 4096 to 16384, as said below
Outputs:
- scored: bfloat16 [4, 16384, 1024], P('group', 'pos')
Inputs may be any that keep to these rules, and one draw needn't show every extreme that they name: `hist_len`: lengths are multiples of 128 and some request has the longest history 4096. `cand_count`: some request has all 16384 candidates live. `user_slot`: each cache slot serves exactly one request.
All inputs are finite; a program needn't handle non-finite values.
Results may differ from a plain program's by a relative error of at most 0.0049.
Values may be sent and summed in bfloat16 or wider, within the bound.
A program may use at most 256 MiB of HBM per device.

v0:
```python
import math

import jax
import jax.numpy as jnp
from jax import lax
from jax.sharding import PartitionSpec as P

HEADS = 8


def body(cand_x, f1_weight, out_weight, kv_cache, user_slot, hist_len, cand_count):
    req_rows, cand_rows, width = cand_x.shape
    hist_rows = kv_cache.shape[1]
    head_size = width // HEADS
    scale = 1.0 / math.sqrt(head_size)
    group_index = lax.axis_index("group")
    pos_index = lax.axis_index("pos")
    mine = group_index * req_rows + jnp.arange(req_rows, dtype=jnp.int32)
    slots = jnp.take(user_slot, mine)
    lengths = jnp.take(hist_len, mine)
    counts = jnp.take(cand_count, mine)
    denom = (lengths + 1).astype(jnp.float32)
    piece = lax.all_gather(kv_cache, "group", axis=0, tiled=True)
    count_rows = piece.shape[0]
    onehot = (slots[:, None] == jnp.arange(count_rows, dtype=jnp.int32)[None, :]).astype(
        jnp.bfloat16
    )
    chosen = jnp.dot(onehot, piece.reshape(count_rows, -1), preferred_element_type=jnp.float32)
    history = chosen.astype(jnp.bfloat16).reshape(
        jnp.zeros((req_rows, hist_rows, 2 * width), jnp.bfloat16).shape
    )
    flat = cand_x.reshape(req_rows * cand_rows, width)
    proj = jax.nn.silu(jnp.dot(flat, f1_weight, preferred_element_type=jnp.float32)).astype(
        jnp.bfloat16
    )
    proj = proj.reshape(req_rows, cand_rows, 4 * width)
    gate = proj[:, :, :width]
    own_value = proj[:, :, width : 2 * width]
    query = proj[:, :, 2 * width : 3 * width]
    own_key = proj[:, :, 3 * width :]

    def attend(query_part, kv_part, first_pos):
        count_k = kv_part.shape[1]
        positions = first_pos + jnp.arange(count_k, dtype=jnp.int32)
        live = positions < lengths[0]
        heads_out = []
        for head in range(HEADS):
            low = head * head_size
            query_h = query_part[0, :, low : low + head_size]
            key_h = kv_part[0, :, low : low + head_size]
            value_h = kv_part[0, :, width + low : width + low + head_size]
            scores = (
                lax.dot_general(
                    query_h, key_h, (((1,), (1,)), ((), ())), preferred_element_type=jnp.float32
                )
                * scale
            )
            weights = jnp.where(live[None, :], jax.nn.silu(scores) / denom[0], 0.0).astype(
                jnp.bfloat16
            )
            heads_out.append(jnp.dot(weights, value_h, preferred_element_type=jnp.float32))
        outputs = [jnp.concatenate(heads_out, axis=-1)]
        return jnp.stack(outputs, axis=0)

    piece = lax.all_gather(history, "pos", axis=1, tiled=True)
    total = piece.shape[1]
    block = 512

    def step(index, acc):
        kv_block = lax.dynamic_slice_in_dim(piece, index * block, block, 1)
        return acc + attend(query, kv_block, index * block)

    attn = lax.fori_loop(
        0, total // block, step, jnp.zeros((req_rows, cand_rows, width), jnp.float32)
    )
    query_heads = query.reshape(req_rows, cand_rows, HEADS, head_size).astype(jnp.float32)
    key_heads = own_key.reshape(req_rows, cand_rows, HEADS, head_size).astype(jnp.float32)
    value_heads = own_value.reshape(req_rows, cand_rows, HEADS, head_size).astype(jnp.float32)
    self_score = jnp.sum(query_heads * key_heads, axis=-1) * scale
    self_weight = (jax.nn.silu(self_score) / denom[:, None, None]).astype(jnp.bfloat16)
    attn = attn + (self_weight.astype(jnp.float32)[:, :, :, None] * value_heads).reshape(
        req_rows, cand_rows, width
    )
    mean = jnp.mean(attn, axis=-1, keepdims=True)
    centered = attn - mean
    var = jnp.mean(centered * centered, axis=-1, keepdims=True)
    normed = centered * lax.rsqrt(var + 1e-05)
    mixed = (normed * gate.astype(jnp.float32)).astype(jnp.bfloat16)
    result = cand_x.astype(jnp.float32) + jnp.dot(
        mixed.reshape(-1, width), out_weight, preferred_element_type=jnp.float32
    ).reshape(req_rows, cand_rows, width)
    cand_ids = pos_index * cand_rows + jnp.arange(cand_rows, dtype=jnp.int32)
    live_c = cand_ids[None, :] < counts[:, None]
    return jnp.where(live_c[:, :, None], result, 0.0).astype(jnp.bfloat16)


def solution(mesh):
    placed = (P("group", "pos", None), P(), P(), P("group", "pos", None), P(), P(), P())
    return jax.shard_map(
        body, mesh=mesh, in_specs=placed, out_specs=P("group", "pos", None), check_vma=False
    )
```

profile of v0, /device:TPU:1, one launch (start us, length us, event | category | flops | bytes accessed | tf_op | source)
XLA Modules:
  0.0 319.8 jit_solution(9769433221367775297)
XLA Ops:
  9.2 33.9 %all-gather.3.cloned.1.call-done = bf16[4,128,2048]{2,1,0:T(8,128)(2,1)} async-done(((bf16[1,128,2048]{2,1,0:T(8,128)(2,1)}), bf16[4,128,2048]{2,1,0:T(8,128)(2,1)}) %all-gather.3.cloned.1.call-update) | async-done | bytes 2097168 | tf_op jit(solution)/shard_map/all_gather | solution.py:23
  43.1 3.2 %copy.15 = bf16[1,4,128,2048]{3,1,2,0:T(4,128)(2,1)S(1)} copy(bf16[1,4,128,2048]{3,2,1,0:T(8,128)(2,1)} %bitcast.246) | data formatting | bytes 4194304
  49.9 9.1 %fusion.120 = bf16[1,512,4096]{2,1,0:T(8,128)(2,1)S(1)} fusion(bf16[1024,4096]{1,0:T(8,128)(2,1)} %param.10, bf16[1,512,1024]{2,1,0:T(8,128)(2,1)} %param.9), kind=kOutput, calls=%fused_computation.139 | convolution fusion | flops 4305453056 | bytes 13631488 | tf_op jit(solution)/shard_map/dot_general | solution.py:33
  69.1 2.8 mul.226
  73.2 48.7 %all-gather.5.cloned.1.call-done = bf16[1,4096,2048]{2,1,0:T(8,128)(2,1)} async-done(((bf16[1,128,2048]{2,1,0:T(8,128)(2,1)}), bf16[1,4096,2048]{2,1,0:T(8,128)(2,1)}) %all-gather.5.cloned.1.call-update) | async-done | bytes 16777232 | tf_op jit(solution)/shard_map/all_gather | solution.py:65
  121.9 181.3 %while.17 = (s32[]{:T(128)}, f32[1,512,1024]{1,2,0:T(8,128)}, s32[1]{0:T(128)}, bf16[1,4096,2048]{2,1,0:T(8,128)(2,1)}, bf16[1,512,1024]{2,1,0:T(8,128)(2,1)S(1)...) while((s32[]{:T(128)}, f32[1,512,1024]{1,2,0:T(8,128)}, ...), condition=%wide.region_1.2_spmd.clone, body=%wide.region_0.1_spmd.clone.sunk | while | flops 1091568640 | bytes 11559377 | solution.py:73
  121.9 2.4 convolution_dynamic-update-slice_fusion.16
  126.6 2.3 convolution_dynamic-update-slice_fusion.18
  128.9 2.4 convolution_dynamic-update-slice_fusion.19
  140.6 3.4 %bitcast_add_fusion.3 = f32[1,512,1024]{1,2,0:T(8,128)} fusion(f32[512,1024]{0,1:T(8,128)} %convolution_dynamic-update-slice_fusion.23, f32[1,512,1024]{1,2,0:T(8,128)} %get-tuple-element.246, pred[]{:T(512)S(6)} %compare.6), kind=kLoop, calls=%fused_computation.clone.1 | loop fusion | flops 1048576 | bytes 6291457 | tf_op jit(solution)/shard_map/while/body/eval_jaxpr/add | solution.py:71
  144.0 2.4 convolution_dynamic-update-slice_fusion.16
  146.4 2.3 convolution_dynamic-update-slice_fusion.17
  148.7 2.3 convolution_dynamic-update-slice_fusion.18
  151.1 2.3 convolution_dynamic-update-slice_fusion.19
  162.7 4.1 %bitcast_add_fusion.3 = f32[1,512,1024]{1,2,0:T(8,128)} fusion(f32[512,1024]{0,1:T(8,128)} %convolution_dynamic-update-slice_fusion.23, f32[1,512,1024]{1,2,0:T(8,128)} %get-tuple-element.246, pred[]{:T(512)S(6)} %compare.6), kind=kLoop, calls=%fused_computation.clone.1 | loop fusion | flops 1048576 | bytes 6291457 | tf_op jit(solution)/shard_map/while/body/eval_jaxpr/add | solution.py:71
  166.8 2.4 convolution_dynamic-update-slice_fusion.16
  169.1 2.3 convolution_dynamic-update-slice_fusion.17
  171.4 2.4 convolution_dynamic-update-slice_fusion.18
  173.8 2.3 convolution_dynamic-update-slice_fusion.19
  178.5 2.3 convolution_dynamic-update-slice_fusion.21
  185.4 4.1 %bitcast_add_fusion.3 = f32[1,512,1024]{1,2,0:T(8,128)} fusion(f32[512,1024]{0,1:T(8,128)} %convolution_dynamic-update-slice_fusion.23, f32[1,512,1024]{1,2,0:T(8,128)} %get-tuple-element.246, pred[]{:T(512)S(6)} %compare.6), kind=kLoop, calls=%fused_computation.clone.1 | loop fusion | flops 1048576 | bytes 6291457 | tf_op jit(solution)/shard_map/while/body/eval_jaxpr/add | solution.py:71
  189.5 2.4 convolution_dynamic-update-slice_fusion.16
  191.9 2.3 convolution_dynamic-update-slice_fusion.17
  194.2 2.3 convolution_dynamic-update-slice_fusion.18
  196.5 2.3 convolution_dynamic-update-slice_fusion.19
  208.2 4.1 %bitcast_add_fusion.3 = f32[1,512,1024]{1,2,0:T(8,128)} fusion(f32[512,1024]{0,1:T(8,128)} %convolution_dynamic-update-slice_fusion.23, f32[1,512,1024]{1,2,0:T(8,128)} %get-tuple-element.246, pred[]{:T(512)S(6)} %compare.6), kind=kLoop, calls=%fused_computation.clone.1 | loop fusion | flops 1048576 | bytes 6291457 | tf_op jit(solution)/shard_map/while/body/eval_jaxpr/add | solution.py:71
  212.3 2.4 convolution_dynamic-update-slice_fusion.16
  214.6 2.3 convolution_dynamic-update-slice_fusion.17
  216.9 2.3 convolution_dynamic-update-slice_fusion.18
  219.3 2.3 convolution_dynamic-update-slice_fusion.19
  230.9 4.1 %bitcast_add_fusion.3 = f32[1,512,1024]{1,2,0:T(8,128)} fusion(f32[512,1024]{0,1:T(8,128)} %convolution_dynamic-update-slice_fusion.23, f32[1,512,1024]{1,2,0:T(8,128)} %get-tuple-element.246, pred[]{:T(512)S(6)} %compare.6), kind=kLoop, calls=%fused_computation.clone.1 | loop fusion | flops 1048576 | bytes 6291457 | tf_op jit(solution)/shard_map/while/body/eval_jaxpr/add | solution.py:71
  235.0 2.4 convolution_dynamic-update-slice_fusion.16
  237.4 2.3 convolution_dynamic-update-slice_fusion.17
  239.7 2.3 convolution_dynamic-update-slice_fusion.18
  242.0 2.3 convolution_dynamic-update-slice_fusion.19
  253.7 4.1 %bitcast_add_fusion.3 = f32[1,512,1024]{1,2,0:T(8,128)} fusion(f32[512,1024]{0,1:T(8,128)} %convolution_dynamic-update-slice_fusion.23, f32[1,512,1024]{1,2,0:T(8,128)} %get-tuple-element.246, pred[]{:T(512)S(6)} %compare.6), kind=kLoop, calls=%fused_computation.clone.1 | loop fusion | flops 1048576 | bytes 6291457 | tf_op jit(solution)/shard_map/while/body/eval_jaxpr/add | solution.py:71
  257.7 2.4 convolution_dynamic-update-slice_fusion.16
  260.1 2.3 convolution_dynamic-update-slice_fusion.17
  262.4 2.3 convolution_dynamic-update-slice_fusion.18
  264.8 2.3 convolution_dynamic-update-slice_fusion.19
  276.4 4.1 %bitcast_add_fusion.3 = f32[1,512,1024]{1,2,0:T(8,128)} fusion(f32[512,1024]{0,1:T(8,128)} %convolution_dynamic-update-slice_fusion.23, f32[1,512,1024]{1,2,0:T(8,128)} %get-tuple-element.246, pred[]{:T(512)S(6)} %compare.6), kind=kLoop, calls=%fused_computation.clone.1 | loop fusion | flops 1048576 | bytes 6291457 | tf_op jit(solution)/shard_map/while/body/eval_jaxpr/add | solution.py:71
  280.5 2.4 convolution_dynamic-update-slice_fusion.16
  285.2 2.3 convolution_dynamic-update-slice_fusion.18
  287.5 2.3 convolution_dynamic-update-slice_fusion.19
  299.2 4.1 %bitcast_add_fusion.3 = f32[1,512,1024]{1,2,0:T(8,128)} fusion(f32[512,1024]{0,1:T(8,128)} %convolution_dynamic-update-slice_fusion.23, f32[1,512,1024]{1,2,0:T(8,128)} %get-tuple-element.246, pred[]{:T(512)S(6)} %compare.6), kind=kLoop, calls=%fused_computation.clone.1 | loop fusion | flops 1048576 | bytes 6291457 | tf_op jit(solution)/shard_map/while/body/eval_jaxpr/add | solution.py:71
  303.2 2.9 copy.14
  306.2 3.0 fusion.136
  310.6 2.4 fusion.122
  (77 shorter events, 93.7 us)
Async XLA Ops:
  6.5 303.0 %copy-start = (bf16[1024,1024]{1,0:T(8,128)(2,1)S(1)}, bf16[1024,1024]{1,0:T(8,128)(2,1)}, u32[]{:S(2)}) copy-start(bf16[1024,1024]{1,0:T(8,128)(2,1)} %param.11) | copy-start | bytes 6291460
  6.5 36.6 %all-gather.3.cloned.1.call-start = ((), (), s32[]{:S(2)}) async-start(), calls=%async_computation | async-start | bytes 2621440 | tf_op jit(solution)/shard_map/all_gather | solution.py:23
  7.3 114.6 %all-gather.5.cloned.1.call-start = ((), (), s32[]{:S(2)}) async-start(), calls=%async_computation.1 | async-start | bytes 17301504 | tf_op jit(solution)/shard_map/all_gather | solution.py:65
  47.6 1.1 copy-start.4
  58.9 1.9 copy-start.1
  69.1 2.8 copy-start.5
  69.1 52.8 %slice-start = ((bf16[1,512,4096]{2,1,0:T(8,128)(2,1)}), bf16[1,512,1024]{2,1,0:T(8,128)(2,1)S(1)}, s32[]{:S(2)}) async-start(bf16[1,512,4096]{2,1,0:T(8,128)(2,1)} %copy-done.1), calls=%async_computation.2 | async-start | bytes 2097152 | tf_op jit(solution)/shard_map/slice | solution.py:39
  306.2 3.8 %copy-start.2 = (bf16[1,512,4096]{2,1,0:T(8,128)(2,1)S(1)}, bf16[1,512,4096]{2,1,0:T(8,128)(2,1)}, u32[]{:S(2)}) copy-start(bf16[1,512,4096]{2,1,0:T(8,128)(2,1)} %copy-done.1) | copy-start | bytes 12582916
  309.2 1.4 copy-start.3
Sparse Core Ops, SparseCore 0:
  9.0 34.0 all-gather.2
  48.8 73.0 all-gather.4
where the time goes:
time: 321 us; the launch traced here: 320 us
  matrix products  162 us (50%)
  waiting for transfers between devices  83.3 us (26%)
  other arithmetic  39.6 us (12%)
  local copies, waits for them, and re-layouts  19.4 us (6%)
  between operations  15.4 us (5%)
    dot_general x64, matrix products, attend(): jnp.dot(weights, value_h, preferred_element_type=jnp.float32)  149 us
    all_gather x1, waiting for transfers between devices, body(): piece = lax.all_gather(history, 'pos', axis=1, tiled=True)  48.7 us
    all_gather x1, waiting for transfers between devices, body(): piece = lax.all_gather(kv_cache, 'group', axis=0, tiled=True)  33.9 us
    add x8, other arithmetic, step(): return acc + attend(query, kv_block, index * block)  31.9 us
    dot_general x1, matrix products, body(): jnp.dot(flat, f1_weight, preferred_element_type=jnp.float32)  9.05 us
    unnamed x14, local copies, waits for them, and re-layouts  7.98 us
  transfers between devices with their start and end apart: 2, of which 2 were waited for; matrix products, arithmetic and copies ran while one was open for 7% of the time, Pallas kernels for 0%

commit v1 on v0

v1 whole, which is shorter than its diff:
```python
import math

import jax
import jax.numpy as jnp
from jax import lax
from jax.experimental import pallas as pl
from jax.experimental.pallas import tpu as pltpu
from jax.sharding import PartitionSpec as P

MESH = pl.DeviceIdType.MESH
HEADS = 8
HD = 128
D = 1024
ROWS = 512
HIST = 128
NQ = 4
R = HIST // NQ
PART = 32 * R
COLS = 256


def silu(v):
    h = 0.5 * v
    return h + h * jnp.tanh(h)


def wait_bytes(ref, sem):
    pltpu.make_async_copy(ref, ref, sem).wait()


def kernel(
    slot_ref, len_ref, count_ref, x_hbm, f1_hbm, ow_hbm, kv_hbm, out_ref,
    xv, f1v, owv, kvin, st1, st2, kvbuf, projv, qbuf, acc, asend, abuf, selfv,
    load_sem, f1_sem, s1s, s1r, s2s, s2r, xs, xr, qs, qr, os, orr,
):
    y = lax.axis_index("group")
    pos = lax.axis_index("pos")
    c = lax.rem(pos, 2)
    z = lax.rem(pos // 2, 4)
    x = pos // 8
    line = z * 2 + c

    def at(xx, zz, cc):
        return (xx * 4 + zz) * 2 + cc

    kv_loads = [
        pltpu.make_async_copy(kv_hbm.at[:, pl.ds(i * D, D)], kvin.at[i], load_sem.at[i]) for i in range(2)
    ]
    for cp in kv_loads:
        cp.start()
    x_load = pltpu.make_async_copy(x_hbm, xv, load_sem.at[2])
    x_load.start()
    f1_loads = {}
    for i in (2, 3, 1, 0):
        cols = pl.ds(i * D, D)
        f1_loads[i] = pltpu.make_async_copy(f1_hbm.at[:, cols], f1v.at[:, cols], f1_sem.at[i])
        f1_loads[i].start()
    ow_load = pltpu.make_async_copy(ow_hbm, owv, load_sem.at[3])
    ow_load.start()

    barrier = pltpu.get_barrier_semaphore()

    def greet(g, p):
        pl.semaphore_signal(barrier, inc=1, device_id=(g, p), device_id_type=MESH)

    for d in range(1, 4):
        greet(lax.rem(y + d, 4), pos)
        greet(y, at(lax.rem(x + d, 4), z, c))
    for dz in range(4):
        for dc in range(2):
            if dz or dc:
                greet(y, at(x, lax.rem(z + dz, 4), lax.rem(c + dc, 2)))
    for yy in range(4):
        for dc in range(2):
            who = (yy, at(x, lax.rem(z + 4 - yy, 4), lax.rem(c + dc, 2)))
            if yy == 0 and dc == 0:
                @pl.when(y != 0)
                def _():
                    greet(*who)
            else:
                greet(*who)

    @pl.when(y == 0)
    def _():
        pl.semaphore_wait(barrier, 20)

    @pl.when(y != 0)
    def _():
        pl.semaphore_wait(barrier, 21)

    for cp in kv_loads:
        cp.wait()

    def pair_cols(yy):
        return pl.ds(pl.multiple_of(lax.rem(z + yy, 4) * 256, 256), 256)

    for q in range(NQ):
        rows = pl.ds(q * R, R)
        for d in (2, 1, 3):
            yy = lax.rem(y + d, 4)
            pltpu.make_async_remote_copy(
                src_ref=kvin.at[:, rows, pair_cols(yy)],
                dst_ref=st1[q].at[y],
                send_sem=s1s,
                recv_sem=s1r.at[q],
                device_id=(yy, pos),
                device_id_type=MESH,
            ).start()
        st1[q][y] = kvin[:, rows, pair_cols(y)]

    def project(i):
        f1_loads[i].wait()

        def tile(n, carry):
            cols = pl.ds(pl.multiple_of(i * D + n * COLS, COLS), COLS)
            v = jnp.dot(xv[...], f1v[:, cols], preferred_element_type=jnp.float32)
            projv[:, cols] = silu(v).astype(jnp.bfloat16)
            return carry

        lax.fori_loop(0, D // COLS, tile, 0)

    x_load.wait()
    project(2)

    def head_cols(base, head):
        return pl.ds(pl.multiple_of(base * D + head * HD, HD), HD)

    for dz in (2, 1, 3, 0):
        for dc in range(2):
            if dz or dc:
                zz, cc = lax.rem(z + dz, 4), lax.rem(c + dc, 2)
                pltpu.make_async_remote_copy(
                    src_ref=projv.at[:, head_cols(2, zz * 2 + cc)],
                    dst_ref=qbuf.at[line],
                    send_sem=qs,
                    recv_sem=qr,
                    device_id=(y, at(x, zz, cc)),
                    device_id_type=MESH,
                ).start()
    qbuf[line] = projv[:, head_cols(2, line)]

    def stage2(q):
        rows = pl.ds(q * R, R)
        wait_bytes(st1[q].at[pl.ds(0, 3)], s1r.at[q])
        for r in range(4):
            s = slot_ref[r]
            live = (pos * HIST < len_ref[r]).astype(jnp.bfloat16)
            both = st1[q][s]
            for cc in range(2):
                st2[r, cc, 0, rows, :] = both[0, :, cc * HD : (cc + 1) * HD]
                st2[r, cc, 1, rows, :] = both[1, :, cc * HD : (cc + 1) * HD] * live
        zz = lax.rem(z + y, 4)
        for d in (2, 1, 3, 0):
            r = lax.rem(y + d, 4)
            for dc in range(2):
                cc = lax.rem(c + dc, 2)
                src = st2.at[r, cc, :, rows, :]
                dst = kvbuf.at[:, q, x, line]

                def remote():
                    pltpu.make_async_remote_copy(
                        src_ref=src,
                        dst_ref=dst,
                        send_sem=s2s,
                        recv_sem=s2r.at[q],
                        device_id=(r, at(x, zz, cc)),
                        device_id_type=MESH,
                    ).start()

                if d == 0 and dc == 0:
                    pl.when(y != 0)(remote)

                    @pl.when(y == 0)
                    def _():
                        pltpu.make_async_copy(src, dst, s2r.at[q]).start()
                else:
                    remote()

    def share(q):
        wait_bytes(kvbuf.at[:, q, x], s2r.at[q])
        for d in (2, 1, 3):
            pltpu.make_async_remote_copy(
                src_ref=kvbuf.at[:, q, x],
                dst_ref=kvbuf.at[:, q, x],
                send_sem=xs,
                recv_sem=xr.at[q],
                device_id=(y, at(lax.rem(x + d, 4), z, c)),
                device_id_type=MESH,
            ).start()

    denom = (len_ref[y] + 1).astype(jnp.float32)
    scale = 1.0 / math.sqrt(HD)

    def own_term():
        def tile(n, carry):
            rows = pl.ds(pl.multiple_of(n * 128, 128), 128)
            for h in range(HEADS):
                lo = h * HD
                qh = projv[rows, 2 * D + lo : 2 * D + lo + HD].astype(jnp.float32)
                kh = projv[rows, 3 * D + lo : 3 * D + lo + HD].astype(jnp.float32)
                vh = projv[rows, D + lo : D + lo + HD].astype(jnp.float32)
                score = jnp.sum(qh * kh, axis=-1, keepdims=True) * scale
                weight = (silu(score) / denom).astype(jnp.bfloat16).astype(jnp.float32)
                selfv[rows, lo : lo + HD] = weight * vh
            return carry

        lax.fori_loop(0, ROWS // 128, tile, 0)

    stage2(0)
    project(3)
    stage2(1)
    share(0)
    project(1)
    stage2(2)
    share(1)
    project(0)
    stage2(3)
    share(2)
    own_term()
    share(3)

    wait_bytes(qbuf.at[pl.ds(0, 7)], qr)

    def attend(q, qv):
        k = kvbuf[0, q].reshape(PART, HD)
        v = kvbuf[1, q].reshape(PART, HD)
        s = lax.dot_general(qv, k, (((1,), (1,)), ((), ())), preferred_element_type=jnp.float32)
        w = silu(s * scale).astype(jnp.bfloat16)
        return jnp.dot(w, v, preferred_element_type=jnp.float32)

    for q in range(NQ - 1):
        wait_bytes(kvbuf.at[:, q, pl.ds(0, 3)], xr.at[q])

        def block(b, carry, q=q):
            part = pl.ds(b * 2, 2)
            o = attend(q, qbuf[part].reshape(2 * ROWS, HD)).reshape(2, ROWS, HD)
            if q == 0:
                acc[part] = o
            else:
                acc[part] += o
            return carry

        lax.fori_loop(0, 4, block, 0)

    wait_bytes(kvbuf.at[:, NQ - 1, pl.ds(0, 3)], xr.at[NQ - 1])

    def last(i, carry):
        zz = lax.rem(z + i // 2 + 1, 4)
        cc = lax.rem(c + i + 1, 2)
        b = zz * 2 + cc
        o = acc[b] + attend(NQ - 1, qbuf[b])
        asend[b] = (o / denom).astype(jnp.bfloat16)

        @pl.when(i < 7)
        def _():
            pltpu.make_async_remote_copy(
                src_ref=asend.at[b],
                dst_ref=abuf.at[line],
                send_sem=os,
                recv_sem=orr,
                device_id=(y, at(x, zz, cc)),
                device_id_type=MESH,
            ).start()

        return carry

    lax.fori_loop(0, 8, last, 0)
    abuf[line] = asend[line]

    ow_load.wait()
    wait_bytes(abuf.at[pl.ds(0, 7)], orr)
    count = count_ref[y]

    def finish(n, carry):
        rows = pl.ds(pl.multiple_of(n * 128, 128), 128)
        attn = jnp.concatenate([abuf[h, rows, :] for h in range(HEADS)], axis=-1).astype(jnp.float32)
        attn = attn + selfv[rows, :]
        mean = jnp.mean(attn, axis=-1, keepdims=True)
        centered = attn - mean
        var = jnp.mean(centered * centered, axis=-1, keepdims=True)
        normed = centered * lax.rsqrt(var + 1e-05)
        mixed = (normed * projv[rows, 0:D].astype(jnp.float32)).astype(jnp.bfloat16)
        result = xv[rows, :].astype(jnp.float32) + jnp.dot(mixed, owv[...], preferred_element_type=jnp.float32)
        ids = pos * ROWS + n * 128 + lax.broadcasted_iota(jnp.int32, (128, 1), 0)
        out_ref[rows, :] = jnp.where(ids < count, result, 0.0).astype(jnp.bfloat16)
        return carry

    lax.fori_loop(0, ROWS // 128, finish, 0)

    for q in range(NQ):
        wait_bytes(st1[q].at[pl.ds(0, 3)], s1s)
    wait_bytes(qbuf.at[pl.ds(0, 7)], qs)

    @pl.when(y == 0)
    def _():
        wait_bytes(st2.at[pl.ds(0, 3)], s2s)
        wait_bytes(st2.at[0, 0], s2s)

    @pl.when(y != 0)
    def _():
        wait_bytes(st2, s2s)

    wait_bytes(kvbuf.at[:, :, pl.ds(0, 3)], xs)
    wait_bytes(abuf.at[pl.ds(0, 7)], os)


def body(cand_x, f1_weight, out_weight, kv_cache, user_slot, hist_len, cand_count):
    bf = jnp.bfloat16
    smem = pl.BlockSpec(memory_space=pltpu.SMEM)
    hbm = pl.BlockSpec(memory_space=pl.ANY)
    dma = pltpu.SemaphoreType.DMA
    out = pl.pallas_call(
        kernel,
        out_shape=jax.ShapeDtypeStruct((ROWS, D), bf),
        in_specs=[smem] * 3 + [hbm] * 4,
        out_specs=pl.BlockSpec(memory_space=pltpu.VMEM),
        scratch_shapes=[
            pltpu.VMEM((ROWS, D), bf),
            pltpu.VMEM((D, 4 * D), bf),
            pltpu.VMEM((D, D), bf),
            pltpu.VMEM((2, HIST, D), bf),
            [pltpu.VMEM((4, 2, R, 2 * HD), bf)] * NQ,
            pltpu.VMEM((4, 2, 2, HIST, HD), bf),
            pltpu.VMEM((2, NQ, 4, 8, R, HD), bf),
            pltpu.VMEM((ROWS, 4 * D), bf),
            pltpu.VMEM((8, ROWS, HD), bf),
            pltpu.VMEM((8, ROWS, HD), jnp.float32),
            pltpu.VMEM((8, ROWS, HD), bf),
            pltpu.VMEM((8, ROWS, HD), bf),
            pltpu.VMEM((ROWS, D), jnp.float32),
            dma((4,)),
            dma((4,)),
            dma,
            dma((NQ,)),
            dma,
            dma((NQ,)),
            dma,
            dma((NQ,)),
            dma,
            dma,
            dma,
            dma,
        ],
        compiler_params=pltpu.CompilerParams(
            collective_id=0, has_side_effects=True, vmem_limit_bytes=60 * 2**20
        ),
    )(
        user_slot, hist_len, cand_count,
        cand_x.reshape(ROWS, D), f1_weight, out_weight, kv_cache.reshape(HIST, 2 * D),
    )
    return out.reshape(1, ROWS, D)


def solution(mesh):
    placed = (P("group", "pos", None), P(), P(), P("group", "pos", None), P(), P(), P())
    return jax.shard_map(
        body, mesh=mesh, in_specs=placed, out_specs=P("group", "pos", None), check_vma=False
    )
```

time: 321 us -> 72.5 us (0.23)
  matrix products: 162 us -> 0 us
  waiting for transfers between devices: 83.3 us -> 0 us
  Pallas kernels: 0 us -> 70.1 us
  other arithmetic: 39.6 us -> 0 us
  local copies, waits for them, and re-layouts: 19.4 us -> 2.26 us
  between operations: 15.4 us -> 0.01 us
    dot_general x67 -> x0, matrix products: 162 us -> none  [the longest x64 149 us: attend(): jnp.dot(weights, value_h, preferred_element_type=jnp.float32)]
    all_gather x2 -> x0, waiting for transfers between devices: 82.6 us -> none  [the longest x1 48.7 us: body(): piece = lax.all_gather(history, 'pos', axis=1, tiled=True)]
    pallas_call x0 -> x1, Pallas kernels: none -> 70.1 us  [body(): pl.pallas_call(kernel, out_shape=jax.ShapeDtypeStruct((ROWS, D), bf), in_...]
    add x8 -> x0, other arithmetic: 31.9 us -> none  [step(): return acc + attend(query, kv_block, index * block)]
    unnamed x14 -> x1, local copies, waits for them, and re-layouts: 7.98 us -> 2.26 us
    reduce_sum x3 -> x0, other arithmetic: 5.57 us -> none  [the longest x1 2.98 us: body(): mean = jnp.mean(attn, axis=-1, keepdims=True)]
    mul x2 -> x0, local copies, waits for them, and re-layouts: 4.79 us -> none  [body(): self_weight.astype(jnp.float32)[:, :, :, None] * value_heads]
  transfers between devices with their start and end apart: 2 -> 0, of which waited for: 2 -> 0; matrix products, arithmetic and copies ran while one was open for 7% -> 0% of each run, Pallas kernels for 0% -> 0%
where the time goes in v1:
time: 72.5 us; the launch traced here: 72.3 us
  Pallas kernels  70.1 us (97%)
  local copies, waits for them, and re-layouts  2.26 us (3%)
    pallas_call x1, Pallas kernels, body(): pl.pallas_call(kernel, out_shape=jax.ShapeDtypeStruct((ROWS, D), bf), in_...  70.1 us
    unnamed x1, local copies, waits for them, and re-layouts  2.26 us

profile of v1, /device:TPU:1, one launch (start us, length us, event | category | flops | bytes accessed | tf_op | source)
XLA Modules:
  0.0 72.3 jit_solution(17382649049842588284)
XLA Ops:
  0.0 70.1 %shard_map.73 = bf16[512,1024]{1,0:T(8,128)(2,1)} custom-call(s32[4]{0:T(128)} %slot_ref.1, s32[4]{0:T(128)} %len_ref.1, s32[4]{0:T(128)} %count_ref.1, bf16[512,1024]{1,0:T(8,128)(2,1)} %bitcast.4, bf16[1024,4096]{1,0:T(8,128)(2,1)} %f1_hbm.1, bf16[1024,1024]{1,0:T(8,128)(2,1)} %ow_hbm.1, bf16[128,2048]{1,0:T(8,128)(2,1)} %bitcast.5), custom_call_target="tpu_custom_call" | custom-call | tf_op jit(solution)/shard_map/pallas_call | solution.py:312
  70.1 2.3 %copy.9 = bf16[1,512,1024]{2,1,0:T(8,128)(2,1)} copy(bf16[1,512,1024]{2,1,0:T(8,128)(2,1)} %bitcast.3) | data formatting | bytes 2097152

commit v2 on v1

--- a/solution.py
+++ b/solution.py
@@ -38,10 +38,20 @@
     c = lax.rem(pos, 2)
     z = lax.rem(pos // 2, 4)
     x = pos // 8
-    line = z * 2 + c
+    chip = x * 4 + z
 
     def at(xx, zz, cc):
         return (xx * 4 + zz) * 2 + cc
+
+    def head_at(xx, zz):
+        a = lax.rem(xx + 4 - zz, 4)
+        return (lax.rem(a, 2) * 2 + lax.rem(xx, 2)) * 2 + a // 2
+
+    mine = head_at(x, z)
+    offsets = [
+        (1 + 2 * c, 1 + 2 * c), (1 + 2 * c, 3 - 2 * c), (2 - 2 * c, 2 * c),
+        (1, 0), (3, 0), (0, 1), (0, 3), (0, 0),
+    ]
 
     kv_loads = [
         pltpu.make_async_copy(kv_hbm.at[:, pl.ds(i * D, D)], kvin.at[i], load_sem.at[i]) for i in range(2)
@@ -65,34 +75,37 @@
 
     for d in range(1, 4):
         greet(lax.rem(y + d, 4), pos)
-        greet(y, at(lax.rem(x + d, 4), z, c))
-    for dz in range(4):
-        for dc in range(2):
-            if dz or dc:
-                greet(y, at(x, lax.rem(z + dz, 4), lax.rem(c + dc, 2)))
+    greet(y, at(x, z, 1 - c))
+    for dx, dz in offsets[:7]:
+        greet(y, at(lax.rem(x + 4 - dx, 4), lax.rem(z + 4 - dz, 4), c))
+        greet(y, at(lax.rem(x + dx, 4), lax.rem(z + dz, 4), c))
     for yy in range(4):
-        for dc in range(2):
-            who = (yy, at(x, lax.rem(z + 4 - yy, 4), lax.rem(c + dc, 2)))
-            if yy == 0 and dc == 0:
-                @pl.when(y != 0)
-                def _():
+        for m in range(2):
+            for n in range(2):
+                dx, dz = yy % 2 + 2 * m, yy // 2 + 2 * n
+                who = (yy, at(lax.rem(x + 4 - dx, 4), lax.rem(z + 4 - dz, 4), c))
+                if yy == 0 and m == 0 and n == 0:
+                    @pl.when(y != 0)
+                    def _():
+                        greet(*who)
+                else:
                     greet(*who)
-            else:
-                greet(*who)
 
     @pl.when(y == 0)
     def _():
-        pl.semaphore_wait(barrier, 20)
+        pl.semaphore_wait(barrier, 33)
 
     @pl.when(y != 0)
     def _():
-        pl.semaphore_wait(barrier, 21)
+        pl.semaphore_wait(barrier, 34)
 
     for cp in kv_loads:
         cp.wait()
 
     def pair_cols(yy):
-        return pl.ds(pl.multiple_of(lax.rem(z + yy, 4) * 256, 256), 256)
+        odd = lax.rem(yy, 2)
+        pair = lax.rem(x + z + odd + yy // 2, 2) * 2 + lax.rem(x + odd, 2)
+        return pl.ds(pl.multiple_of(pair * 256, 256), 256)
 
     for q in range(NQ):
         rows = pl.ds(q * R, R)
@@ -125,19 +138,17 @@
     def head_cols(base, head):
         return pl.ds(pl.multiple_of(base * D + head * HD, HD), HD)
 
-    for dz in (2, 1, 3, 0):
-        for dc in range(2):
-            if dz or dc:
-                zz, cc = lax.rem(z + dz, 4), lax.rem(c + dc, 2)
-                pltpu.make_async_remote_copy(
-                    src_ref=projv.at[:, head_cols(2, zz * 2 + cc)],
-                    dst_ref=qbuf.at[line],
-                    send_sem=qs,
-                    recv_sem=qr,
-                    device_id=(y, at(x, zz, cc)),
-                    device_id_type=MESH,
-                ).start()
-    qbuf[line] = projv[:, head_cols(2, line)]
+    for k in range(7):
+        xx, zz = lax.rem(x + offsets[k][0], 4), lax.rem(z + offsets[k][1], 4)
+        pltpu.make_async_remote_copy(
+            src_ref=projv.at[:, head_cols(2, head_at(xx, zz))],
+            dst_ref=qbuf.at[k],
+            send_sem=qs,
+            recv_sem=qr,
+            device_id=(y, at(xx, zz, c)),
+            device_id_type=MESH,
+        ).start()
+    qbuf[7] = projv[:, head_cols(2, mine)]
 
     def stage2(q):
         rows = pl.ds(q * R, R)
@@ -149,44 +160,45 @@
             for cc in range(2):
                 st2[r, cc, 0, rows, :] = both[0, :, cc * HD : (cc + 1) * HD]
                 st2[r, cc, 1, rows, :] = both[1, :, cc * HD : (cc + 1) * HD] * live
-        zz = lax.rem(z + y, 4)
         for d in (2, 1, 3, 0):
             r = lax.rem(y + d, 4)
-            for dc in range(2):
-                cc = lax.rem(c + dc, 2)
-                src = st2.at[r, cc, :, rows, :]
-                dst = kvbuf.at[:, q, x, line]
-
-                def remote():
-                    pltpu.make_async_remote_copy(
-                        src_ref=src,
-                        dst_ref=dst,
-                        send_sem=s2s,
-                        recv_sem=s2r.at[q],
-                        device_id=(r, at(x, zz, cc)),
-                        device_id_type=MESH,
-                    ).start()
-
-                if d == 0 and dc == 0:
-                    pl.when(y != 0)(remote)
-
-                    @pl.when(y == 0)
-                    def _():
-                        pltpu.make_async_copy(src, dst, s2r.at[q]).start()
-                else:
-                    remote()
+            for m in (1, 0):
+                for n in (1, 0):
+                    xx = lax.rem(x + lax.rem(y, 2) + 2 * m, 4)
+                    zz = lax.rem(z + y // 2 + 2 * n, 4)
+                    j = lax.rem(xx + 4 - zz, 4) // 2
+                    src = st2.at[r, j, :, rows, :]
+                    dst = kvbuf.at[:, q, c, chip]
+
+                    def remote():
+                        pltpu.make_async_remote_copy(
+                            src_ref=src,
+                            dst_ref=dst,
+                            send_sem=s2s,
+                            recv_sem=s2r.at[q],
+                            device_id=(r, at(xx, zz, c)),
+                            device_id_type=MESH,
+                        ).start()
+
+                    if d == 0 and m == 0 and n == 0:
+                        pl.when(y != 0)(remote)
+
+                        @pl.when(y == 0)
+                        def _():
+                            pltpu.make_async_copy(src, dst, s2r.at[q]).start()
+                    else:
+                        remote()
 
     def share(q):
-        wait_bytes(kvbuf.at[:, q, x], s2r.at[q])
-        for d in (2, 1, 3):
-            pltpu.make_async_remote_copy(
-                src_ref=kvbuf.at[:, q, x],
-                dst_ref=kvbuf.at[:, q, x],
-                send_sem=xs,
-                recv_sem=xr.at[q],
-                device_id=(y, at(lax.rem(x + d, 4), z, c)),
-                device_id_type=MESH,
-            ).start()
+        wait_bytes(kvbuf.at[:, q, c], s2r.at[q])
+        pltpu.make_async_remote_copy(
+            src_ref=kvbuf.at[:, q, c],
+            dst_ref=kvbuf.at[:, q, c],
+            send_sem=xs,
+            recv_sem=xr.at[q],
+            device_id=(y, at(x, z, 1 - c)),
+            device_id_type=MESH,
+        ).start()
 
     denom = (len_ref[y] + 1).astype(jnp.float32)
     scale = 1.0 / math.sqrt(HD)
@@ -229,7 +241,7 @@
         return jnp.dot(w, v, preferred_element_type=jnp.float32)
 
     for q in range(NQ - 1):
-        wait_bytes(kvbuf.at[:, q, pl.ds(0, 3)], xr.at[q])
+        wait_bytes(kvbuf.at[:, q, 1 - c], xr.at[q])
 
         def block(b, carry, q=q):
             part = pl.ds(b * 2, 2)
@@ -242,30 +254,22 @@
 
         lax.fori_loop(0, 4, block, 0)
 
-    wait_bytes(kvbuf.at[:, NQ - 1, pl.ds(0, 3)], xr.at[NQ - 1])
-
-    def last(i, carry):
-        zz = lax.rem(z + i // 2 + 1, 4)
-        cc = lax.rem(c + i + 1, 2)
-        b = zz * 2 + cc
-        o = acc[b] + attend(NQ - 1, qbuf[b])
-        asend[b] = (o / denom).astype(jnp.bfloat16)
-
-        @pl.when(i < 7)
-        def _():
+    wait_bytes(kvbuf.at[:, NQ - 1, 1 - c], xr.at[NQ - 1])
+
+    for k in range(8):
+        o = (acc[k] + attend(NQ - 1, qbuf[k])) / denom
+        if k == 7:
+            abuf[mine] = o.astype(jnp.bfloat16)
+        else:
+            asend[k] = o.astype(jnp.bfloat16)
             pltpu.make_async_remote_copy(
-                src_ref=asend.at[b],
-                dst_ref=abuf.at[line],
+                src_ref=asend.at[k],
+                dst_ref=abuf.at[mine],
                 send_sem=os,
                 recv_sem=orr,
-                device_id=(y, at(x, zz, cc)),
+                device_id=(y, at(lax.rem(x + 4 - offsets[k][0], 4), lax.rem(z + 4 - offsets[k][1], 4), c)),
                 device_id_type=MESH,
             ).start()
-
-        return carry
-
-    lax.fori_loop(0, 8, last, 0)
-    abuf[line] = asend[line]
 
     ow_load.wait()
     wait_bytes(abuf.at[pl.ds(0, 7)], orr)
@@ -294,13 +298,17 @@
     @pl.when(y == 0)
     def _():
         wait_bytes(st2.at[pl.ds(0, 3)], s2s)
+        wait_bytes(st2.at[pl.ds(0, 3)], s2s)
+        wait_bytes(st2.at[0, 0], s2s)
+        wait_bytes(st2.at[0, 0], s2s)
         wait_bytes(st2.at[0, 0], s2s)
 
     @pl.when(y != 0)
     def _():
         wait_bytes(st2, s2s)
-
-    wait_bytes(kvbuf.at[:, :, pl.ds(0, 3)], xs)
+        wait_bytes(st2, s2s)
+
+    wait_bytes(kvbuf.at[:, :, 0], xs)
     wait_bytes(abuf.at[pl.ds(0, 7)], os)
 
 
@@ -321,11 +329,11 @@
             pltpu.VMEM((2, HIST, D), bf),
             [pltpu.VMEM((4, 2, R, 2 * HD), bf)] * NQ,
             pltpu.VMEM((4, 2, 2, HIST, HD), bf),
-            pltpu.VMEM((2, NQ, 4, 8, R, HD), bf),
+            pltpu.VMEM((2, NQ, 2, 16, R, HD), bf),
             pltpu.VMEM((ROWS, 4 * D), bf),
             pltpu.VMEM((8, ROWS, HD), bf),
             pltpu.VMEM((8, ROWS, HD), jnp.float32),
-            pltpu.VMEM((8, ROWS, HD), bf),
+            pltpu.VMEM((7, ROWS, HD), bf),
             pltpu.VMEM((8, ROWS, HD), bf),
             pltpu.VMEM((ROWS, D), jnp.float32),
             dma((4,)),

time: 72.5 us -> 70.7 us (0.975)
  Pallas kernels: 70.1 us -> 68.3 us
    pallas_call x1, Pallas kernels: 70.1 us -> 68.3 us  [body(): pl.pallas_call(kernel, out_shape=jax.ShapeDtypeStruct((ROWS, D), bf), in_...]
where the time goes in v2:
time: 70.7 us; the launch traced here: 70.6 us
  Pallas kernels  68.3 us (97%)
  local copies, waits for them, and re-layouts  2.26 us (3%)
    pallas_call x1, Pallas kernels, body(): pl.pallas_call(kernel, out_shape=jax.ShapeDtypeStruct((ROWS, D), bf), in_...  68.3 us
    unnamed x1, local copies, waits for them, and re-layouts  2.26 us

profile of v2, /device:TPU:1, one launch (start us, length us, event | category | flops | bytes accessed | tf_op | source)
XLA Modules:
  0.0 70.6 jit_solution(11696131288959933175)
XLA Ops:
  0.0 68.3 %shard_map.73 = bf16[512,1024]{1,0:T(8,128)(2,1)} custom-call(s32[4]{0:T(128)} %slot_ref.1, s32[4]{0:T(128)} %len_ref.1, s32[4]{0:T(128)} %count_ref.1, bf16[512,1024]{1,0:T(8,128)(2,1)} %bitcast.4, bf16[1024,4096]{1,0:T(8,128)(2,1)} %f1_hbm.1, bf16[1024,1024]{1,0:T(8,128)(2,1)} %ow_hbm.1, bf16[128,2048]{1,0:T(8,128)(2,1)} %bitcast.5), custom_call_target="tpu_custom_call" | custom-call | tf_op jit(solution)/shard_map/pallas_call | solution.py:320
  68.3 2.3 %copy.9 = bf16[1,512,1024]{2,1,0:T(8,128)(2,1)} copy(bf16[1,512,1024]{2,1,0:T(8,128)(2,1)} %bitcast.3) | data formatting | bytes 2097152

commit v3 on v2

--- a/solution.py
+++ b/solution.py
@@ -15,8 +15,12 @@
 HIST = 128
 NQ = 4
 R = HIST // NQ
-PART = 32 * R
+SPANS = ((0, 1), (1, 2), (2, 4))
+NS = len(SPANS)
+LAST = NS - 1
+WIDE = [(b - a) * R for a, b in SPANS]
 COLS = 256
+SPREAD = (10, 2, 8, 6, 14, 9, 11, 5, 7, 13, 15, 1, 3, 4, 12, 0)
 
 
 def silu(v):
@@ -30,8 +34,9 @@
 
 def kernel(
     slot_ref, len_ref, count_ref, x_hbm, f1_hbm, ow_hbm, kv_hbm, out_ref,
-    xv, f1v, owv, kvin, st1, st2, kvbuf, projv, qbuf, acc, asend, abuf, selfv,
-    load_sem, f1_sem, s1s, s1r, s2s, s2r, xs, xr, qs, qr, os, orr,
+    xv, f1v, owv, kvin, st1, st2, sel, kvbuf, projv, qbuf, acc, asend, abuf, selfv,
+    load_sem, f1_sem, s1s, s1r, s2s, s2r, s3s, s3r, xs, xr, qs, qr, os, orr,
+    in_plane,
 ):
     y = lax.axis_index("group")
     pos = lax.axis_index("pos")
@@ -70,42 +75,29 @@
 
     barrier = pltpu.get_barrier_semaphore()
 
-    def greet(g, p):
-        pl.semaphore_signal(barrier, inc=1, device_id=(g, p), device_id_type=MESH)
-
+    def greet(sem, g, p):
+        pl.semaphore_signal(sem, inc=1, device_id=(g, p), device_id_type=MESH)
+
+    def greet_x(sem):
+        for d in range(1, 4):
+            greet(sem, y, at(lax.rem(x + d, 4), z, c))
+
+    def greet_y(sem):
+        for d in range(1, 4):
+            greet(sem, lax.rem(y + d, 4), pos)
+
+    greet_y(barrier)
+    greet_x(barrier)
     for d in range(1, 4):
-        greet(lax.rem(y + d, 4), pos)
-    greet(y, at(x, z, 1 - c))
-    for dx, dz in offsets[:7]:
-        greet(y, at(lax.rem(x + 4 - dx, 4), lax.rem(z + 4 - dz, 4), c))
-        greet(y, at(lax.rem(x + dx, 4), lax.rem(z + dz, 4), c))
-    for yy in range(4):
-        for m in range(2):
-            for n in range(2):
-                dx, dz = yy % 2 + 2 * m, yy // 2 + 2 * n
-                who = (yy, at(lax.rem(x + 4 - dx, 4), lax.rem(z + 4 - dz, 4), c))
-                if yy == 0 and m == 0 and n == 0:
-                    @pl.when(y != 0)
-                    def _():
-                        greet(*who)
-                else:
-                    greet(*who)
-
-    @pl.when(y == 0)
-    def _():
-        pl.semaphore_wait(barrier, 33)
-
-    @pl.when(y != 0)
-    def _():
-        pl.semaphore_wait(barrier, 34)
+        greet(barrier, y, at(x, lax.rem(z + d, 4), c))
+    greet(barrier, y, at(x, z, 1 - c))
+    pl.semaphore_wait(barrier, 10)
 
     for cp in kv_loads:
         cp.wait()
 
     def pair_cols(yy):
-        odd = lax.rem(yy, 2)
-        pair = lax.rem(x + z + odd + yy // 2, 2) * 2 + lax.rem(x + odd, 2)
-        return pl.ds(pl.multiple_of(pair * 256, 256), 256)
+        return pl.ds(pl.multiple_of(yy * 256, 256), 256)
 
     for q in range(NQ):
         rows = pl.ds(q * R, R)
@@ -121,6 +113,9 @@
             ).start()
         st1[q][y] = kvin[:, rows, pair_cols(y)]
 
+    greet_x(in_plane)
+    pl.semaphore_wait(in_plane, 3)
+
     def project(i):
         f1_loads[i].wait()
 
@@ -151,51 +146,55 @@
     qbuf[7] = projv[:, head_cols(2, mine)]
 
     def stage2(q):
-        rows = pl.ds(q * R, R)
         wait_bytes(st1[q].at[pl.ds(0, 3)], s1r.at[q])
+        g = [i for i in range(NS) if SPANS[i][0] <= q < SPANS[i][1]][0]
+        rows = pl.ds((q - SPANS[g][0]) * R, R)
         for r in range(4):
             s = slot_ref[r]
             live = (pos * HIST < len_ref[r]).astype(jnp.bfloat16)
             both = st1[q][s]
-            for cc in range(2):
-                st2[r, cc, 0, rows, :] = both[0, :, cc * HD : (cc + 1) * HD]
-                st2[r, cc, 1, rows, :] = both[1, :, cc * HD : (cc + 1) * HD] * live
-        for d in (2, 1, 3, 0):
+            for j in range(2):
+                st2[r, q, j, 0] = both[0, :, j * HD : (j + 1) * HD]
+                st2[r, q, j, 1] = both[1, :, j * HD : (j + 1) * HD] * live
+        for d in (2, 1, 3):
             r = lax.rem(y + d, 4)
-            for m in (1, 0):
-                for n in (1, 0):
-                    xx = lax.rem(x + lax.rem(y, 2) + 2 * m, 4)
-                    zz = lax.rem(z + y // 2 + 2 * n, 4)
-                    j = lax.rem(xx + 4 - zz, 4) // 2
-                    src = st2.at[r, j, :, rows, :]
-                    dst = kvbuf.at[:, q, c, chip]
-
-                    def remote():
-                        pltpu.make_async_remote_copy(
-                            src_ref=src,
-                            dst_ref=dst,
-                            send_sem=s2s,
-                            recv_sem=s2r.at[q],
-                            device_id=(r, at(xx, zz, c)),
-                            device_id_type=MESH,
-                        ).start()
-
-                    if d == 0 and m == 0 and n == 0:
-                        pl.when(y != 0)(remote)
-
-                        @pl.when(y == 0)
-                        def _():
-                            pltpu.make_async_copy(src, dst, s2r.at[q]).start()
-                    else:
-                        remote()
-
-    def share(q):
-        wait_bytes(kvbuf.at[:, q, c], s2r.at[q])
+            pltpu.make_async_remote_copy(
+                src_ref=st2.at[r, q],
+                dst_ref=sel[g].at[y, :, :, rows, :],
+                send_sem=s2s,
+                recv_sem=s2r.at[q],
+                device_id=(r, pos),
+                device_id_type=MESH,
+            ).start()
+        sel[g][y, :, :, rows, :] = st2[y, q]
+
+    def stage3(g):
+        for q in range(*SPANS[g]):
+            wait_bytes(st2.at[pl.ds(0, 3), q], s2r.at[q])
+        for d in SPREAD:
+            xx, zz = lax.rem(x + d // 4, 4), lax.rem(z + d % 4, 4)
+            h = head_at(xx, zz)
+            src = sel[g].at[h // 2, lax.rem(h, 2)]
+            dst = kvbuf[g].at[:, c, chip]
+            if d == 0:
+                pltpu.make_async_copy(src, dst, s3r.at[g]).start()
+            else:
+                pltpu.make_async_remote_copy(
+                    src_ref=src,
+                    dst_ref=dst,
+                    send_sem=s3s,
+                    recv_sem=s3r.at[g],
+                    device_id=(y, at(xx, zz, c)),
+                    device_id_type=MESH,
+                ).start()
+
+    def share(g):
+        wait_bytes(kvbuf[g].at[:, c], s3r.at[g])
         pltpu.make_async_remote_copy(
-            src_ref=kvbuf.at[:, q, c],
-            dst_ref=kvbuf.at[:, q, c],
+            src_ref=kvbuf[g].at[:, c],
+            dst_ref=kvbuf[g].at[:, c],
             send_sem=xs,
-            recv_sem=xr.at[q],
+            recv_sem=xr.at[g],
             device_id=(y, at(x, z, 1 - c)),
             device_id_type=MESH,
         ).start()
@@ -218,58 +217,79 @@
 
         lax.fori_loop(0, ROWS // 128, tile, 0)
 
+    pieces = [lambda: project(3), lambda: project(1), lambda: project(0), own_term]
+    ready = [b for a, b in SPANS]
     stage2(0)
-    project(3)
-    stage2(1)
-    share(0)
-    project(1)
-    stage2(2)
-    share(1)
-    project(0)
-    stage2(3)
-    share(2)
-    own_term()
-    share(3)
-
-    wait_bytes(qbuf.at[pl.ds(0, 7)], qr)
-
-    def attend(q, qv):
-        k = kvbuf[0, q].reshape(PART, HD)
-        v = kvbuf[1, q].reshape(PART, HD)
+    done = 0
+    for q in range(1, NQ):
+        stage2(q)
+        for piece in pieces[(q - 1) * 4 // (NQ - 1) : q * 4 // (NQ - 1)]:
+            piece()
+        if ready[done] <= q:
+            stage3(done)
+            done += 1
+    while done < NS:
+        stage3(done)
+        done += 1
+
+    def attend(g, half, qv):
+        k = kvbuf[g][0, half].reshape(16 * WIDE[g], HD)
+        v = kvbuf[g][1, half].reshape(16 * WIDE[g], HD)
         s = lax.dot_general(qv, k, (((1,), (1,)), ((), ())), preferred_element_type=jnp.float32)
         w = silu(s * scale).astype(jnp.bfloat16)
         return jnp.dot(w, v, preferred_element_type=jnp.float32)
 
-    for q in range(NQ - 1):
-        wait_bytes(kvbuf.at[:, q, 1 - c], xr.at[q])
-
-        def block(b, carry, q=q):
-            part = pl.ds(b * 2, 2)
-            o = attend(q, qbuf[part].reshape(2 * ROWS, HD)).reshape(2, ROWS, HD)
-            if q == 0:
+    def attend_all(g, half, first):
+        count = 8 if WIDE[g] == R else 4
+
+        def block(b, carry):
+            part = pl.ds(b * count, count)
+            o = attend(g, half, qbuf[part].reshape(count * ROWS, HD)).reshape(count, ROWS, HD)
+            if first:
                 acc[part] = o
             else:
                 acc[part] += o
             return carry
 
-        lax.fori_loop(0, 4, block, 0)
-
-    wait_bytes(kvbuf.at[:, NQ - 1, 1 - c], xr.at[NQ - 1])
-
-    for k in range(8):
-        o = (acc[k] + attend(NQ - 1, qbuf[k])) / denom
-        if k == 7:
-            abuf[mine] = o.astype(jnp.bfloat16)
-        else:
-            asend[k] = o.astype(jnp.bfloat16)
+        lax.fori_loop(0, 8 // count, block, 0)
+
+    for g in range(LAST):
+        share(g)
+        if g == 0:
+            wait_bytes(qbuf.at[pl.ds(0, 7)], qr)
+        attend_all(g, c, g == 0)
+        wait_bytes(kvbuf[g].at[:, 1 - c], xr.at[g])
+        attend_all(g, 1 - c, False)
+
+    share(LAST)
+    wait_bytes(kvbuf[LAST].at[:, 1 - c], xr.at[LAST])
+    steps_x = sum(v * 4**i for i, v in enumerate((1, 1, 2, 1, 3, 0, 0, 0)))
+    steps_x = steps_x + c * (sum(v * 4**i for i, v in enumerate((3, 3, 0, 1, 3, 0, 0, 0))) - steps_x)
+    steps_z = sum(v * 4**i for i, v in enumerate((1, 3, 0, 0, 0, 1, 3, 0)))
+    steps_z = steps_z + c * (sum(v * 4**i for i, v in enumerate((3, 1, 2, 0, 0, 1, 3, 0))) - steps_z)
+
+    def last(k, place):
+        qv = qbuf[k]
+        o = (acc[k] + attend(LAST, 0, qv) + attend(LAST, 1, qv)) / denom
+        asend[k] = o.astype(jnp.bfloat16)
+        xx = lax.rem(x + 4 - lax.rem(steps_x // place, 4), 4)
+        zz = lax.rem(z + 4 - lax.rem(steps_z // place, 4), 4)
+
+        @pl.when(k < 7)
+        def _():
             pltpu.make_async_remote_copy(
                 src_ref=asend.at[k],
                 dst_ref=abuf.at[mine],
                 send_sem=os,
                 recv_sem=orr,
-                device_id=(y, at(lax.rem(x + 4 - offsets[k][0], 4), lax.rem(z + 4 - offsets[k][1], 4), c)),
+                device_id=(y, at(xx, zz, c)),
                 device_id_type=MESH,
             ).start()
+
+        return place * 4
+
+    lax.fori_loop(0, 8, last, 1)
+    abuf[mine] = asend[7]
 
     ow_load.wait()
     wait_bytes(abuf.at[pl.ds(0, 7)], orr)
@@ -295,20 +315,10 @@
         wait_bytes(st1[q].at[pl.ds(0, 3)], s1s)
     wait_bytes(qbuf.at[pl.ds(0, 7)], qs)
 
-    @pl.when(y == 0)
-    def _():
-        wait_bytes(st2.at[pl.ds(0, 3)], s2s)
-        wait_bytes(st2.at[pl.ds(0, 3)], s2s)
-        wait_bytes(st2.at[0, 0], s2s)
-        wait_bytes(st2.at[0, 0], s2s)
-        wait_bytes(st2.at[0, 0], s2s)
-
-    @pl.when(y != 0)
-    def _():
-        wait_bytes(st2, s2s)
-        wait_bytes(st2, s2s)
-
-    wait_bytes(kvbuf.at[:, :, 0], xs)
+    wait_bytes(st2.at[pl.ds(0, 3)], s2s)
+    for g in range(NS):
+        wait_bytes(kvbuf[g].at[:, 0, pl.ds(0, 15)], s3s)
+        wait_bytes(kvbuf[g].at[:, 0], xs)
     wait_bytes(abuf.at[pl.ds(0, 7)], os)
 
 
@@ -328,12 +338,13 @@
             pltpu.VMEM((D, D), bf),
             pltpu.VMEM((2, HIST, D), bf),
             [pltpu.VMEM((4, 2, R, 2 * HD), bf)] * NQ,
-            pltpu.VMEM((4, 2, 2, HIST, HD), bf),
-            pltpu.VMEM((2, NQ, 2, 16, R, HD), bf),
+            pltpu.VMEM((4, NQ, 2, 2, R, HD), bf),
+            [pltpu.VMEM((4, 2, 2, w, HD), bf) for w in WIDE],
+            [pltpu.VMEM((2, 2, 16, w, HD), bf) for w in WIDE],
             pltpu.VMEM((ROWS, 4 * D), bf),
             pltpu.VMEM((8, ROWS, HD), bf),
             pltpu.VMEM((8, ROWS, HD), jnp.float32),
-            pltpu.VMEM((7, ROWS, HD), bf),
+            pltpu.VMEM((8, ROWS, HD), bf),
             pltpu.VMEM((8, ROWS, HD), bf),
             pltpu.VMEM((ROWS, D), jnp.float32),
             dma((4,)),
@@ -343,11 +354,14 @@
             dma,
             dma((NQ,)),
             dma,
-            dma((NQ,)),
-            dma,
-            dma,
-            dma,
-            dma,
+            dma((NS,)),
+            dma,
+            dma((NS,)),
+            dma,
+            dma,
+            dma,
+            dma,
+            pltpu.SemaphoreType.REGULAR,
         ],
         compiler_params=pltpu.CompilerParams(
             collective_id=0, has_side_effects=True, vmem_limit_bytes=60 * 2**20

time: 70.7 us -> 57.1 us (0.81)
  Pallas kernels: 68.3 us -> 54.6 us
    pallas_call x1, Pallas kernels: 68.3 us -> 54.6 us  [body(): pl.pallas_call(kernel, out_shape=jax.ShapeDtypeStruct((ROWS, D), bf), in_...]
where the time goes in v3:
time: 57.1 us; the launch traced here: 56.9 us
  Pallas kernels  54.6 us (96%)
  local copies, waits for them, and re-layouts  2.26 us (4%)
    pallas_call x1, Pallas kernels, body(): pl.pallas_call(kernel, out_shape=jax.ShapeDtypeStruct((ROWS, D), bf), in_...  54.6 us
    unnamed x1, local copies, waits for them, and re-layouts  2.26 us

profile of v3, /device:TPU:1, one launch (start us, length us, event | category | flops | bytes accessed | tf_op | source)
XLA Modules:
  0.0 56.9 jit_solution(984111072742461543)
XLA Ops:
  0.0 54.6 %shard_map.73 = bf16[512,1024]{1,0:T(8,128)(2,1)} custom-call(s32[4]{0:T(128)} %slot_ref.1, s32[4]{0:T(128)} %len_ref.1, s32[4]{0:T(128)} %count_ref.1, bf16[512,1024]{1,0:T(8,128)(2,1)} %bitcast.4, bf16[1024,4096]{1,0:T(8,128)(2,1)} %f1_hbm.1, bf16[1024,1024]{1,0:T(8,128)(2,1)} %ow_hbm.1, bf16[128,2048]{1,0:T(8,128)(2,1)} %bitcast.5), custom_call_target="tpu_custom_call" | custom-call | tf_op jit(solution)/shard_map/pallas_call | solution.py:330
  54.6 2.3 %copy.9 = bf16[1,512,1024]{2,1,0:T(8,128)(2,1)} copy(bf16[1,512,1024]{2,1,0:T(8,128)(2,1)} %bitcast.3) | data formatting | bytes 2097152

commit v4 on v3

--- a/solution.py
+++ b/solution.py
@@ -33,7 +33,7 @@
 
 
 def kernel(
-    slot_ref, len_ref, count_ref, x_hbm, f1_hbm, ow_hbm, kv_hbm, out_ref,
+    slot_ref, len_ref, x_hbm, f1_hbm, ow_hbm, kv_hbm, out_ref,
     xv, f1v, owv, kvin, st1, st2, sel, kvbuf, projv, qbuf, acc, asend, abuf, selfv,
     load_sem, f1_sem, s1s, s1r, s2s, s2r, s3s, s3r, xs, xr, qs, qr, os, orr,
     in_plane,
@@ -217,20 +217,17 @@
 
         lax.fori_loop(0, ROWS // 128, tile, 0)
 
-    pieces = [lambda: project(3), lambda: project(1), lambda: project(0), own_term]
-    ready = [b for a, b in SPANS]
     stage2(0)
-    done = 0
-    for q in range(1, NQ):
-        stage2(q)
-        for piece in pieces[(q - 1) * 4 // (NQ - 1) : q * 4 // (NQ - 1)]:
-            piece()
-        if ready[done] <= q:
-            stage3(done)
-            done += 1
-    while done < NS:
-        stage3(done)
-        done += 1
+    stage2(1)
+    project(3)
+    project(1)
+    stage2(2)
+    project(0)
+    stage3(0)
+    stage2(3)
+    own_term()
+    stage3(1)
+    stage3(2)
 
     def attend(g, half, qv):
         k = kvbuf[g][0, half].reshape(16 * WIDE[g], HD)
@@ -293,7 +290,6 @@
 
     ow_load.wait()
     wait_bytes(abuf.at[pl.ds(0, 7)], orr)
-    count = count_ref[y]
 
     def finish(n, carry):
         rows = pl.ds(pl.multiple_of(n * 128, 128), 128)
@@ -305,8 +301,7 @@
         normed = centered * lax.rsqrt(var + 1e-05)
         mixed = (normed * projv[rows, 0:D].astype(jnp.float32)).astype(jnp.bfloat16)
         result = xv[rows, :].astype(jnp.float32) + jnp.dot(mixed, owv[...], preferred_element_type=jnp.float32)
-        ids = pos * ROWS + n * 128 + lax.broadcasted_iota(jnp.int32, (128, 1), 0)
-        out_ref[rows, :] = jnp.where(ids < count, result, 0.0).astype(jnp.bfloat16)
+        out_ref[rows, :] = result.astype(jnp.bfloat16)
         return carry
 
     lax.fori_loop(0, ROWS // 128, finish, 0)
@@ -330,7 +325,7 @@
     out = pl.pallas_call(
         kernel,
         out_shape=jax.ShapeDtypeStruct((ROWS, D), bf),
-        in_specs=[smem] * 3 + [hbm] * 4,
+        in_specs=[smem] * 2 + [hbm] * 4,
         out_specs=pl.BlockSpec(memory_space=pltpu.VMEM),
         scratch_shapes=[
             pltpu.VMEM((ROWS, D), bf),
@@ -367,10 +362,12 @@
             collective_id=0, has_side_effects=True, vmem_limit_bytes=60 * 2**20
         ),
     )(
-        user_slot, hist_len, cand_count,
+        user_slot, hist_len,
         cand_x.reshape(ROWS, D), f1_weight, out_weight, kv_cache.reshape(HIST, 2 * D),
     )
-    return out.reshape(1, ROWS, D)
+    count = cand_count[lax.axis_index("group")]
+    ids = lax.axis_index("pos") * ROWS + jnp.arange(ROWS, dtype=jnp.int32)
+    return jnp.where((ids < count)[None, :, None], out.reshape(1, ROWS, D), jnp.bfloat16(0))
 
 
 def solution(mesh):

time: 57.1 us -> 61.4 us (1.075)
  other arithmetic: 0 us -> 2.99 us
  Pallas kernels: 54.6 us -> 57 us
  local copies, waits for them, and re-layouts: 2.26 us -> 1.24 us
    pallas_call x1, Pallas kernels: 54.6 us -> 57 us  [body(): pl.pallas_call(kernel, out_shape=jax.ShapeDtypeStruct((ROWS, D), bf), in_...]
    select_n x0 -> x1, other arithmetic: none -> 2.34 us  [body(): jnp.where((ids < count)[None, :, None], out.reshape(1, ROWS, D), jnp.bflo...]
    unnamed x1 -> x0, local copies, waits for them, and re-layouts: 2.26 us -> none
    dynamic_slice x0 -> x1, local copies, waits for them, and re-layouts: none -> 1.24 us  [body(): count = cand_count[lax.axis_index('group')]]
    lt x0 -> x1, other arithmetic: none -> 0.65 us  [body(): ids < count]
where the time goes in v4:
time: 61.4 us; the launch traced here: 61.3 us
  Pallas kernels  57 us (93%)
  other arithmetic  2.99 us (5%)
  local copies, waits for them, and re-layouts  1.24 us (2%)
    pallas_call x1, Pallas kernels, body(): pl.pallas_call(kernel, out_shape=jax.ShapeDtypeStruct((ROWS, D), bf), in_...  57 us
    select_n x1, other arithmetic, body(): jnp.where((ids < count)[None, :, None], out.reshape(1, ROWS, D), jnp.bflo...  2.34 us
    dynamic_slice x1, local copies, waits for them, and re-layouts, body(): count = cand_count[lax.axis_index('group')]  1.24 us

profile of v4, /device:TPU:1, one launch (start us, length us, event | category | flops | bytes accessed | tf_op | source)
XLA Modules:
  0.0 61.3 jit_solution(15455326245421241017)
XLA Ops:
  0.0 1.2 %dynamic_slice.3 = s32[1]{0:T(128)} dynamic-slice(s32[4]{0:T(128)} %param.13, s32[]{:T(128)S(6)} %select_n.10), dynamic_slice_sizes={1} | dynamic-slice | bytes 12 | tf_op jit(solution)/shard_map/dynamic_slice | solution.py:368
  1.2 0.7 %add_compare_fusion = pred[512]{0:T(512)(128)(4,1)S(1)} fusion(s32[]{:T(128)} %bitcast, s32[]{:T(128)S(6)} %mul.3), kind=kLoop, calls=%fused_computation.1 | loop fusion | flops 1024 | bytes 520 | tf_op jit(solution)/shard_map/lt | solution.py:370
  1.9 57.0 %shard_map.73 = bf16[512,1024]{1,0:T(8,128)(2,1)} custom-call(s32[4]{0:T(128)} %slot_ref.1, s32[4]{0:T(128)} %len_ref.1, bf16[512,1024]{1,0:T(8,128)(2,1)} %bitcast.5, bf16[1024,4096]{1,0:T(8,128)(2,1)} %f1_hbm.1, bf16[1024,1024]{1,0:T(8,128)(2,1)} %ow_hbm.1, bf16[128,2048]{1,0:T(8,128)(2,1)} %bitcast.6), custom_call_target="tpu_custom_call" | custom-call | tf_op jit(solution)/shard_map/pallas_call | solution.py:325
  58.9 2.3 %select_bitcast_fusion = bf16[1,512,1024]{2,1,0:T(8,128)(2,1)} fusion(bf16[512,1024]{1,0:T(8,128)(2,1)} %shard_map.73, pred[512]{0:T(512)(128)(4,1)S(1)} %add_compare_fusion), kind=kLoop, calls=%fused_computation | loop fusion | flops 524288 | bytes 2097664 | tf_op jit(solution)/shard_map/jit(_where)/select_n | solution.py:370

commit v5 on v4

--- a/solution.py
+++ b/solution.py
@@ -33,7 +33,7 @@
 
 
 def kernel(
-    slot_ref, len_ref, x_hbm, f1_hbm, ow_hbm, kv_hbm, out_ref,
+    slot_ref, len_ref, count_ref, x_hbm, f1_hbm, ow_hbm, kv_hbm, out_ref,
     xv, f1v, owv, kvin, st1, st2, sel, kvbuf, projv, qbuf, acc, asend, abuf, selfv,
     load_sem, f1_sem, s1s, s1r, s2s, s2r, s3s, s3r, xs, xr, qs, qr, os, orr,
     in_plane,
@@ -91,6 +91,19 @@
     for d in range(1, 4):
         greet(barrier, y, at(x, lax.rem(z + d, 4), c))
     greet(barrier, y, at(x, z, 1 - c))
+    def project(i):
+        f1_loads[i].wait()
+
+        def tile(n, carry):
+            cols = pl.ds(pl.multiple_of(i * D + n * COLS, COLS), COLS)
+            v = jnp.dot(xv[...], f1v[:, cols], preferred_element_type=jnp.float32)
+            projv[:, cols] = silu(v).astype(jnp.bfloat16)
+            return carry
+
+        lax.fori_loop(0, D // COLS, tile, 0)
+
+    x_load.wait()
+    project(2)
     pl.semaphore_wait(barrier, 10)
 
     for cp in kv_loads:
@@ -114,21 +127,9 @@
         st1[q][y] = kvin[:, rows, pair_cols(y)]
 
     greet_x(in_plane)
+    project(3)
     pl.semaphore_wait(in_plane, 3)
 
-    def project(i):
-        f1_loads[i].wait()
-
-        def tile(n, carry):
-            cols = pl.ds(pl.multiple_of(i * D + n * COLS, COLS), COLS)
-            v = jnp.dot(xv[...], f1v[:, cols], preferred_element_type=jnp.float32)
-            projv[:, cols] = silu(v).astype(jnp.bfloat16)
-            return carry
-
-        lax.fori_loop(0, D // COLS, tile, 0)
-
-    x_load.wait()
-    project(2)
 
     def head_cols(base, head):
         return pl.ds(pl.multiple_of(base * D + head * HD, HD), HD)
@@ -219,14 +220,13 @@
 
     stage2(0)
     stage2(1)
-    project(3)
     project(1)
+    stage3(0)
     stage2(2)
     project(0)
-    stage3(0)
+    stage3(1)
     stage2(3)
     own_term()
-    stage3(1)
     stage3(2)
 
     def attend(g, half, qv):
@@ -290,6 +290,7 @@
 
     ow_load.wait()
     wait_bytes(abuf.at[pl.ds(0, 7)], orr)
+    count = count_ref[y]
 
     def finish(n, carry):
         rows = pl.ds(pl.multiple_of(n * 128, 128), 128)
@@ -301,7 +302,8 @@
         normed = centered * lax.rsqrt(var + 1e-05)
         mixed = (normed * projv[rows, 0:D].astype(jnp.float32)).astype(jnp.bfloat16)
         result = xv[rows, :].astype(jnp.float32) + jnp.dot(mixed, owv[...], preferred_element_type=jnp.float32)
-        out_ref[rows, :] = result.astype(jnp.bfloat16)
+        ids = pos * ROWS + n * 128 + lax.broadcasted_iota(jnp.int32, (128, 1), 0)
+        out_ref[rows, :] = jnp.where(ids < count, result, 0.0).astype(jnp.bfloat16)
         return carry
 
     lax.fori_loop(0, ROWS // 128, finish, 0)
@@ -325,7 +327,7 @@
     out = pl.pallas_call(
         kernel,
         out_shape=jax.ShapeDtypeStruct((ROWS, D), bf),
-        in_specs=[smem] * 2 + [hbm] * 4,
+        in_specs=[smem] * 3 + [hbm] * 4,
         out_specs=pl.BlockSpec(memory_space=pltpu.VMEM),
         scratch_shapes=[
             pltpu.VMEM((ROWS, D), bf),
@@ -362,12 +364,10 @@
             collective_id=0, has_side_effects=True, vmem_limit_bytes=60 * 2**20
         ),
     )(
-        user_slot, hist_len,
+        user_slot, hist_len, cand_count,
         cand_x.reshape(ROWS, D), f1_weight, out_weight, kv_cache.reshape(HIST, 2 * D),
     )
-    count = cand_count[lax.axis_index("group")]
-    ids = lax.axis_index("pos") * ROWS + jnp.arange(ROWS, dtype=jnp.int32)
-    return jnp.where((ids < count)[None, :, None], out.reshape(1, ROWS, D), jnp.bfloat16(0))
+    return out.reshape(1, ROWS, D)
 
 
 def solution(mesh):

time: 61.4 us -> 58.9 us (0.959)
  other arithmetic: 2.99 us -> 0 us
  local copies, waits for them, and re-layouts: 1.24 us -> 2.26 us
    select_n x1 -> x0, other arithmetic: 2.34 us -> none  [body(): jnp.where((ids < count)[None, :, None], out.reshape(1, ROWS, D), jnp.bflo...]
    unnamed x0 -> x1, local copies, waits for them, and re-layouts: none -> 2.26 us
    dynamic_slice x1 -> x0, local copies, waits for them, and re-layouts: 1.24 us -> none  [body(): count = cand_count[lax.axis_index('group')]]
    lt x1 -> x0, other arithmetic: 0.65 us -> none  [body(): ids < count]
where the time goes in v5:
time: 58.9 us; the launch traced here: 58.8 us
  Pallas kernels  56.5 us (96%)
  local copies, waits for them, and re-layouts  2.26 us (4%)
    pallas_call x1, Pallas kernels, body(): pl.pallas_call(kernel, out_shape=jax.ShapeDtypeStruct((ROWS, D), bf), in_...  56.5 us
    unnamed x1, local copies, waits for them, and re-layouts  2.26 us

profile of v5, /device:TPU:1, one launch (start us, length us, event | category | flops | bytes accessed | tf_op | source)
XLA Modules:
  0.0 58.8 jit_solution(8018987374345543145)
XLA Ops:
  0.0 56.5 %shard_map.73 = bf16[512,1024]{1,0:T(8,128)(2,1)} custom-call(s32[4]{0:T(128)} %slot_ref.1, s32[4]{0:T(128)} %len_ref.1, s32[4]{0:T(128)} %count_ref.1, bf16[512,1024]{1,0:T(8,128)(2,1)} %bitcast.4, bf16[1024,4096]{1,0:T(8,128)(2,1)} %f1_hbm.1, bf16[1024,1024]{1,0:T(8,128)(2,1)} %ow_hbm.1, bf16[128,2048]{1,0:T(8,128)(2,1)} %bitcast.5), custom_call_target="tpu_custom_call" | custom-call | tf_op jit(solution)/shard_map/pallas_call | solution.py:327
  56.5 2.3 %copy.9 = bf16[1,512,1024]{2,1,0:T(8,128)(2,1)} copy(bf16[1,512,1024]{2,1,0:T(8,128)(2,1)} %bitcast.3) | data formatting | bytes 2097152

commit v6 on v3

--- a/solution.py
+++ b/solution.py
@@ -114,7 +114,6 @@
         st1[q][y] = kvin[:, rows, pair_cols(y)]
 
     greet_x(in_plane)
-    pl.semaphore_wait(in_plane, 3)
 
     def project(i):
         f1_loads[i].wait()
@@ -129,6 +128,7 @@
 
     x_load.wait()
     project(2)
+    pl.semaphore_wait(in_plane, 3)
 
     def head_cols(base, head):
         return pl.ds(pl.multiple_of(base * D + head * HD, HD), HD)
@@ -149,23 +149,23 @@
         wait_bytes(st1[q].at[pl.ds(0, 3)], s1r.at[q])
         g = [i for i in range(NS) if SPANS[i][0] <= q < SPANS[i][1]][0]
         rows = pl.ds((q - SPANS[g][0]) * R, R)
-        for r in range(4):
+        for d in (2, 1, 3, 0):
+            r = lax.rem(y + d, 4)
             s = slot_ref[r]
             live = (pos * HIST < len_ref[r]).astype(jnp.bfloat16)
             both = st1[q][s]
             for j in range(2):
                 st2[r, q, j, 0] = both[0, :, j * HD : (j + 1) * HD]
                 st2[r, q, j, 1] = both[1, :, j * HD : (j + 1) * HD] * live
-        for d in (2, 1, 3):
-            r = lax.rem(y + d, 4)
-            pltpu.make_async_remote_copy(
-                src_ref=st2.at[r, q],
-                dst_ref=sel[g].at[y, :, :, rows, :],
-                send_sem=s2s,
-                recv_sem=s2r.at[q],
-                device_id=(r, pos),
-                device_id_type=MESH,
-            ).start()
+            if d:
+                pltpu.make_async_remote_copy(
+                    src_ref=st2.at[r, q],
+                    dst_ref=sel[g].at[y, :, :, rows, :],
+                    send_sem=s2s,
+                    recv_sem=s2r.at[q],
+                    device_id=(r, pos),
+                    device_id_type=MESH,
+                ).start()
         sel[g][y, :, :, rows, :] = st2[y, q]
 
     def stage3(g):

time: 57.1 us -> 56.6 us (level)
  no operation moved by 1% of the time
where the time goes in v6:
time: 56.6 us; the launch traced here: 56.5 us
  Pallas kernels  54.2 us (96%)
  local copies, waits for them, and re-layouts  2.26 us (4%)
    pallas_call x1, Pallas kernels, body(): pl.pallas_call(kernel, out_shape=jax.ShapeDtypeStruct((ROWS, D), bf), in_...  54.2 us
    unnamed x1, local copies, waits for them, and re-layouts  2.26 us

profile of v6, /device:TPU:1, one launch (start us, length us, event | category | flops | bytes accessed | tf_op | source)
XLA Modules:
  0.0 56.5 jit_solution(6437769417840260716)
XLA Ops:
  0.0 54.2 %shard_map.73 = bf16[512,1024]{1,0:T(8,128)(2,1)} custom-call(s32[4]{0:T(128)} %slot_ref.1, s32[4]{0:T(128)} %len_ref.1, s32[4]{0:T(128)} %count_ref.1, bf16[512,1024]{1,0:T(8,128)(2,1)} %bitcast.4, bf16[1024,4096]{1,0:T(8,128)(2,1)} %f1_hbm.1, bf16[1024,1024]{1,0:T(8,128)(2,1)} %ow_hbm.1, bf16[128,2048]{1,0:T(8,128)(2,1)} %bitcast.5), custom_call_target="tpu_custom_call" | custom-call | tf_op jit(solution)/shard_map/pallas_call | solution.py:330
  54.2 2.3 %copy.9 = bf16[1,512,1024]{2,1,0:T(8,128)(2,1)} copy(bf16[1,512,1024]{2,1,0:T(8,128)(2,1)} %bitcast.3) | data formatting | bytes 2097152

commit v7 on v6

--- a/solution.py
+++ b/solution.py
@@ -262,15 +262,19 @@
         attend_all(g, 1 - c, False)
 
     share(LAST)
+    acc[0:4] += attend(LAST, c, qbuf[0:4].reshape(4 * ROWS, HD)).reshape(4, ROWS, HD)
     wait_bytes(kvbuf[LAST].at[:, 1 - c], xr.at[LAST])
     steps_x = sum(v * 4**i for i, v in enumerate((1, 1, 2, 1, 3, 0, 0, 0)))
     steps_x = steps_x + c * (sum(v * 4**i for i, v in enumerate((3, 3, 0, 1, 3, 0, 0, 0))) - steps_x)
     steps_z = sum(v * 4**i for i, v in enumerate((1, 3, 0, 0, 0, 1, 3, 0)))
     steps_z = steps_z + c * (sum(v * 4**i for i, v in enumerate((3, 1, 2, 0, 0, 1, 3, 0))) - steps_z)
 
-    def last(k, place):
+    def last(k, place, both):
         qv = qbuf[k]
-        o = (acc[k] + attend(LAST, 0, qv) + attend(LAST, 1, qv)) / denom
+        o = acc[k] + attend(LAST, 1 - c, qv)
+        if both:
+            o = o + attend(LAST, c, qv)
+        o = o / denom
         asend[k] = o.astype(jnp.bfloat16)
         xx = lax.rem(x + 4 - lax.rem(steps_x // place, 4), 4)
         zz = lax.rem(z + 4 - lax.rem(steps_z // place, 4), 4)
@@ -288,7 +292,8 @@
 
         return place * 4
 
-    lax.fori_loop(0, 8, last, 1)
+    place = lax.fori_loop(0, 4, lambda k, p: last(k, p, False), 1)
+    lax.fori_loop(4, 8, lambda k, p: last(k, p, True), place)
     abuf[mine] = asend[7]
 
     ow_load.wait()

time: 56.6 us -> 54.3 us (0.959); the launches traced: 56.5 us -> 53.5 us
  Pallas kernels: 54.2 us -> 51.2 us
    pallas_call x1, Pallas kernels: 54.2 us -> 51.2 us  [body(): pl.pallas_call(kernel, out_shape=jax.ShapeDtypeStruct((ROWS, D), bf), in_...]
where the time goes in v7:
time: 54.3 us; the launch traced here: 53.5 us
  Pallas kernels  51.2 us (94%)
  local copies, waits for them, and re-layouts  2.26 us (4%)
    pallas_call x1, Pallas kernels, body(): pl.pallas_call(kernel, out_shape=jax.ShapeDtypeStruct((ROWS, D), bf), in_...  51.2 us
    unnamed x1, local copies, waits for them, and re-layouts  2.26 us

profile of v7, /device:TPU:1, one launch (start us, length us, event | category | flops | bytes accessed | tf_op | source)
XLA Modules:
  0.0 53.5 jit_solution(11676470103431529462)
XLA Ops:
  0.0 51.2 %shard_map.73 = bf16[512,1024]{1,0:T(8,128)(2,1)} custom-call(s32[4]{0:T(128)} %slot_ref.1, s32[4]{0:T(128)} %len_ref.1, s32[4]{0:T(128)} %count_ref.1, bf16[512,1024]{1,0:T(8,128)(2,1)} %bitcast.4, bf16[1024,4096]{1,0:T(8,128)(2,1)} %f1_hbm.1, bf16[1024,1024]{1,0:T(8,128)(2,1)} %ow_hbm.1, bf16[128,2048]{1,0:T(8,128)(2,1)} %bitcast.5), custom_call_target="tpu_custom_call" | custom-call | tf_op jit(solution)/shard_map/pallas_call | solution.py:335
  51.2 2.3 %copy.9 = bf16[1,512,1024]{2,1,0:T(8,128)(2,1)} copy(bf16[1,512,1024]{2,1,0:T(8,128)(2,1)} %bitcast.3) | data formatting | bytes 2097152
